TPU v7x, 256 devices: a whole 4x4x8 slice. The times are simulated.
256 devices in a mesh: blocks: 64 (over z, x, core), section: 4 (over y).
Axes of the slice: x: 4, y: 4, z: 8, core: 2. Of those that a mesh axis runs over, the one named last changes fastest.
Arguments:
- features: bfloat16 [256, 32, 4096], P(('blocks', 'section')), may hold values from -6 to 6
- grad_pool: bfloat16 [256, 32, 4096], P(('blocks', 'section')), may hold values from -6 to 6
- grad_skip: bfloat16 [256, 32, 4096], P(('blocks', 'section')), may hold values from -6 to 6
- conv_one: bfloat16 [27, 32, 32], replicated, may hold values from -0.21875 to 0.21875
- conv_two: bfloat16 [27, 32, 32], replicated, may hold values from -0.21875 to 0.21875
- block_links: int32 [256, 6], P(('blocks', 'section')), may hold values from -1 to 255, as said below
- block_positions: int32 [256, 3], P(('blocks', 'section')), may hold values from 0 to 4095
- dropout_seed: int32 [1], replicated, may hold values from 0 to 1048575
Outputs:
- encoded: bfloat16 [256, 32, 4096], P(('blocks', 'section'))
- grad_features: bfloat16 [256, 32, 4096], P(('blocks', 'section'))
- grad_conv_one: float32 [27, 32, 32], replicated
- grad_conv_two: float32 [27, 32, 32], replicated
Inputs may be any that keep to these rules, and one draw needn't show every extreme that they name: `block_links`: links are mutual: if entry 2k+1 (the + face along axis k) of block a is b, then entry 2k of block b is a, and the reverse. A block never names itself, and every block named is held by the same device as the naming block or by the device one index before or after it along blocks+section, the last and the first device counting as neighbours.
All inputs are finite; a program needn't handle non-finite values.
Results may differ from a plain program's by a relative error of at most 0.0059.
Values may be sent and summed in bfloat16 or wider, within the bound.
A program may use at most 192 MiB of HBM per device.

v0:
```python
import math

import jax
import jax.numpy as jnp
import numpy as np
from jax import lax
from jax.sharding import PartitionSpec as P

C = 32
EDGE = 16


keep_factor = 1024.0 / 819.0


def from_behind(block, axis, distance):
    devices = range(lax.axis_size(axis))
    route = [((i - distance) % len(devices), i) for i in devices]
    return lax.ppermute(block, axis, route)


def flat_faces(field):
    number = field.shape[0]
    plane = EDGE * EDGE
    volume = EDGE**3
    slabs = field.reshape(number, C, EDGE, plane)
    minus_x = field[:, :, :plane]
    plus_x = field[:, :, volume - plane :]
    minus_y = slabs[:, :, :, :EDGE].reshape(number, C, plane)
    plus_y = slabs[:, :, :, plane - EDGE :].reshape(number, C, plane)
    minus_z = field[:, :, 0::EDGE]
    plus_z = field[:, :, EDGE - 1 :: EDGE]
    return jnp.stack([minus_x, plus_x, minus_y, plus_y, minus_z, plus_z], axis=1)


def local_rims(local_layers, from_prev, from_next, block_links, my_index, device_count):
    per_device = local_layers.shape[0]
    face_pool = jnp.concatenate([from_prev, local_layers, from_next], axis=0)
    opposite = jnp.bitwise_xor(jnp.arange(6, dtype=jnp.int32), 1)[None, :]
    owner_device = block_links // per_device
    index_gap = (owner_device - my_index) % device_count
    source_slot = jnp.where(index_gap == 0, 1, jnp.where(index_gap == 1, 2, 0))
    pool_row = jnp.where(block_links >= 0, source_slot * per_device + block_links % per_device, 0)
    picked = face_pool[pool_row, opposite]
    return jnp.where((block_links >= 0)[:, :, None, None], picked, jnp.zeros_like(picked))


def spread_rims(rims):
    number = rims.shape[0]
    volume = EDGE**3
    spread_x = [jnp.tile(rims[:, face], (1, 1, EDGE)) for face in (0, 1)]
    spread_y = [
        jnp.tile(rims[:, face].reshape(number, C, EDGE, EDGE), (1, 1, 1, EDGE)).reshape(
            number, C, volume
        )
        for face in (2, 3)
    ]
    spread_z = [jnp.repeat(rims[:, face], EDGE, axis=2) for face in (4, 5)]
    return spread_x + spread_y + spread_z


def sliding_flattened(field, amount):
    volume = field.shape[-1]
    if amount == 0:
        return field
    pad_shape = field.shape[:-1] + (abs(amount),)
    zeros_pad = jnp.zeros(pad_shape, field.dtype)
    if amount > 0:
        return jnp.concatenate([field[..., amount:], zeros_pad], axis=-1)
    return jnp.concatenate([zeros_pad, field[..., : volume + amount]], axis=-1)


def offset_tables():
    plane = EDGE * EDGE
    volume = EDGE**3
    ruler = np.arange(volume)
    places = [ruler // plane, ruler // EDGE % EDGE, ruler % EDGE]
    strides = [plane, EDGE, 1]
    tables = []
    for offset in range(27):
        steps = [offset // 9 - 1, offset // 3 % 3 - 1, offset % 3 - 1]
        moved = steps[0] * plane + steps[1] * EDGE + steps[2]
        fits = [
            (places[axis_id] + steps[axis_id] >= 0) & (places[axis_id] + steps[axis_id] < EDGE)
            for axis_id in range(3)
        ]
        inside = fits[0] & fits[1] & fits[2]
        faces = []
        for axis_id in range(3):
            if steps[axis_id] != 0:
                others = [fits[other] for other in range(3) if other != axis_id]
                chosen = ~fits[axis_id] & others[0] & others[1]
                face = 2 * axis_id + (1 if steps[axis_id] > 0 else 0)
                faces.append((face, chosen, moved - steps[axis_id] * strides[axis_id]))
        tables.append((moved, inside, faces))
    return tables


def window_of(field, spread, table):
    moved, inside, faces = table
    result = jnp.where(
        jnp.asarray(inside)[None, None, :],
        sliding_flattened(field, moved),
        jnp.zeros((), field.dtype),
    )
    for face, chosen, amount in faces:
        result = jnp.where(
            jnp.asarray(chosen)[None, None, :], sliding_flattened(spread[face], amount), result
        )
    return result


def convolve(field, spread, kernel, incoming_gradient):
    number = field.shape[0]
    tables = offset_tables()
    summed = None
    pieces = []
    for group in range(3):
        stacked_tiles = jnp.stack(
            [
                window_of(field, spread, tables[offset])
                for offset in range(9 * group, 9 * group + 9)
            ],
            axis=1,
        )
        stacked_tiles = stacked_tiles.reshape(number, 9 * C, EDGE**3)
        if kernel is not None:
            weight_matrix = jnp.transpose(kernel[9 * group : 9 * group + 9], (1, 0, 2)).reshape(
                C, 9 * C
            )
            partial_value = jnp.einsum(
                "cr,xrq->xcq", weight_matrix, stacked_tiles, preferred_element_type=jnp.float32
            )
            summed = partial_value if summed is None else summed + partial_value
        if incoming_gradient is not None:
            product = jnp.einsum(
                "lfj,lpj->fp", incoming_gradient, stacked_tiles, preferred_element_type=jnp.float32
            )
            pieces.append(jnp.transpose(product.reshape(C, 9, C), (1, 0, 2)))
    grads = jnp.concatenate(pieces, axis=0) if incoming_gradient is not None else None
    return (summed, grads)


def mirrored_kernel(kernel):
    return jnp.transpose(kernel[::-1], (0, 2, 1))


def keep_scale(block_positions, dropout_seed):
    plane = EDGE * EDGE
    ruler = jnp.arange(EDGE**3, dtype=jnp.int32)
    global_x = block_positions[:, 0][:, None, None] * EDGE + (ruler // plane)[None, None, :]
    global_y = block_positions[:, 1][:, None, None] * EDGE + (ruler // EDGE % EDGE)[None, None, :]
    global_z = block_positions[:, 2][:, None, None] * EDGE + (ruler % EDGE)[None, None, :]
    channel = jnp.arange(C, dtype=jnp.int32)[None, :, None]
    hashed = jnp.bitwise_xor(global_x * jnp.int32(73856093), global_y * jnp.int32(19349663))
    hashed = jnp.bitwise_xor(hashed, global_z * jnp.int32(83492791))
    hashed = jnp.bitwise_xor(hashed, channel * jnp.int32(1103515245))
    hashed = jnp.bitwise_xor(hashed, dropout_seed[0] * jnp.int32(668265263))
    hashed = jnp.bitwise_xor(hashed, lax.shift_right_logical(hashed, jnp.int32(13)))
    hashed = hashed * jnp.int32(1274126177)
    hashed = jnp.bitwise_xor(hashed, lax.shift_right_logical(hashed, jnp.int32(16)))
    kept_mask = jnp.bitwise_and(hashed, jnp.int32(1023)) >= 205
    return jnp.where(kept_mask, jnp.float32(keep_factor), jnp.float32(0.0))


def trade_faces(layers):
    from_prev = from_behind(layers, ("blocks", "section"), 1)
    from_next = from_behind(layers, ("blocks", "section"), -1)
    return (from_prev, from_next)


def local(
    features, grad_pool, grad_skip, conv_one, conv_two, block_links, block_positions, dropout_seed
):
    device_count = lax.axis_size(("blocks", "section"))
    my_index = lax.axis_index(("blocks", "section"))
    per_device = features.shape[0]
    norm_factor = 1.0 / math.sqrt(per_device * device_count * EDGE**3)
    input_layers = flat_faces(features)
    upstream = (grad_pool.astype(jnp.float32) + grad_skip.astype(jnp.float32)).astype(jnp.bfloat16)
    in_prev, in_next = trade_faces(input_layers)
    spread_in = spread_rims(
        local_rims(input_layers, in_prev, in_next, block_links, my_index, device_count)
    )
    pre, unused_one = convolve(features, spread_in, conv_one, None)
    keep = keep_scale(block_positions, dropout_seed)
    dropped = (jax.nn.silu(pre) * keep).astype(jnp.bfloat16)
    dropped_layers = flat_faces(dropped)
    drop_prev, drop_next = trade_faces(dropped_layers)
    spread_drop = spread_rims(
        local_rims(dropped_layers, drop_prev, drop_next, block_links, my_index, device_count)
    )
    encoded_sum, partial_two = convolve(dropped, spread_drop, conv_two, upstream)
    encoded = encoded_sum.astype(jnp.bfloat16)
    partial_two = partial_two * norm_factor
    upstream_layers = flat_faces(upstream)
    up_prev, up_next = trade_faces(upstream_layers)
    upward_spread = spread_rims(
        local_rims(upstream_layers, up_prev, up_next, block_links, my_index, device_count)
    )
    back, unused_two = convolve(upstream, upward_spread, mirrored_kernel(conv_two), None)
    logistic = jax.nn.sigmoid(pre)
    inner = (back * keep * logistic * (1.0 + pre * (1.0 - logistic))).astype(jnp.bfloat16)
    unused_three, partial_one = convolve(features, spread_in, None, inner)
    partial_one = partial_one * norm_factor
    grad_conv_one, grad_conv_two = lax.psum((partial_one, partial_two), ("blocks", "section"))
    inner_layers = flat_faces(inner)
    inner_prev, inner_next = trade_faces(inner_layers)
    spread_inner = spread_rims(
        local_rims(inner_layers, inner_prev, inner_next, block_links, my_index, device_count)
    )
    grad_sum, unused_four = convolve(inner, spread_inner, mirrored_kernel(conv_one), None)
    grad_features = grad_sum.astype(jnp.bfloat16)
    return (encoded, grad_features, grad_conv_one, grad_conv_two)


def solution(mesh):
    in_specs = (
        P(("blocks", "section"), None, None),
        P(("blocks", "section"), None, None),
        P(("blocks", "section"), None, None),
        P(),
        P(),
        P(("blocks", "section"), None),
        P(("blocks", "section"), None),
        P(),
    )
    out_specs = (
        P(("blocks", "section"), None, None),
        P(("blocks", "section"), None, None),
        P(),
        P(),
    )
    return jax.shard_map(local, mesh=mesh, in_specs=in_specs, out_specs=out_specs, check_vma=False)
```

profile of v0, /device:TPU:1, one launch (start us, length us, event | category | flops | bytes accessed | tf_op | source)
XLA Modules:
  0.0 552.4 jit_solution(3824552230405607602)
XLA Ops:
  10.3 2.2 collective-permute-start.4
  12.5 2.1 collective-permute-start.5
  16.7 3.1 collective-permute-start.1
  75.3 1.5 copy.705
  88.5 1.5 copy.617
  93.0 1.9 copy.711
  114.6 1.7 constant_dynamic-update-slice_fusion.74
  129.7 1.6 fusion.40
  138.6 3.0 collective-permute-start.3
  141.6 2.2 fusion.225
  143.8 1.6 convolution_add_fusion.3
  153.7 3.3 collective-permute-start.7
  179.6 1.8 fusion.28
  181.4 1.8 fusion.25
  183.2 1.8 fusion.22
  203.0 1.5 copy.653
  207.4 1.5 copy.744
  254.4 1.8 fusion.37
  261.1 1.8 fusion.34
  270.0 1.8 fusion.31
  273.0 2.4 fusion.226
  281.9 259.8 %all-reduce.299.cloned.1.call-done = (f32[27,32,32]{2,1,0:T(8,128)}, f32[27,32,32]{2,1,0:T(8,128)}) async-done(((f32[27,32,32]{2,1,0:T(8,128)}, f32[27,32,32]{2,1,0:T(8,128)}), (f32[27,32,32]{2,1,0:T(8,128)}, f32[27,32,32]{2,1,0:T(8,128)})) %all-reduce.299.cloned.1.call-update) | async-done | bytes 221200 | tf_op jit(solution)/shard_map/psum | solution.py:206
  541.7 1.8 copy.906
  543.5 1.8 copy.907
  (1309 shorter events, 223.0 us)
Async XLA Ops:
  7.2 7.5 %copy-start = (bf16[1,32,4096]{2,1,0:T(8,128)(2,1)S(1)}, bf16[1,32,4096]{2,1,0:T(8,128)(2,1)}, u32[]{:S(2)}) copy-start(bf16[1,32,4096]{2,1,0:T(8,128)(2,1)} %param.413) | copy-start | bytes 786436
  7.2 534.5 %all-reduce.299.cloned.1.call-start = ((), (), s32[]{:S(2)}) async-start(), calls=%async_computation | async-start | bytes 1769472 | tf_op jit(solution)/shard_map/psum | solution.py:206
  10.3 41.2 %collective-permute-start.4 = (bf16[1,6,32,256]{3,2,1,0:T(8,128)(2,1)S(1)}, bf16[1,6,32,256]{3,2,1,0:T(8,128)(2,1)S(1)}, u32[]{:S(2)}, u32[]{:S(2)}) collective-permute-start(bf16[1,6,32,256]{3,2,1,0:T(8,128)(2,1)S(1)} %constant_dynamic-update-slice_fusion.66), channel_id=1, source_target_pairs={{255,0},{0,1},{1,2},{2,3},{3,4},{4,5},{5,6},{6,7},{7,8},{8,9},{9,1... | collective-permute-start | bytes 294920 | tf_op jit(solution)/shard_map/ppermute | solution.py:19
  12.5 39.0 %collective-permute-start.5 = (bf16[1,6,32,256]{3,2,1,0:T(8,128)(2,1)S(1)}, bf16[1,6,32,256]{3,2,1,0:T(8,128)(2,1)S(1)}, u32[]{:S(2)}, u32[]{:S(2)}) collective-permute-start(bf16[1,6,32,256]{3,2,1,0:T(8,128)(2,1)S(1)} %constant_dynamic-update-slice_fusion.66), channel_id=1, source_target_pairs={{1,0},{2,1},{3,2},{4,3},{5,4},{6,5},{7,6},{8,7},{9,8},{10,9},{11,1... | collective-permute-start | bytes 294920 | tf_op jit(solution)/shard_map/ppermute | solution.py:19
  16.6 35.6 %collective-permute-start = (bf16[1,6,32,256]{3,2,1,0:T(8,128)(2,1)S(1)}, bf16[1,6,32,256]{3,2,1,0:T(8,128)(2,1)S(1)}, u32[]{:S(2)}, u32[]{:S(2)}) collective-permute-start(bf16[1,6,32,256]{3,2,1,0:T(8,128)(2,1)S(1)} %constant_dynamic-update-slice_fusion), channel_id=1, source_target_pairs={{255,0},{0,1},{1,2},{2,3},{3,4},{4,5},{5,6},{6,7},{7,8},{8,9},{9,1... | collective-permute-start | bytes 294920 | tf_op jit(solution)/shard_map/ppermute | solution.py:19
  16.7 35.5 %collective-permute-start.1 = (bf16[1,6,32,256]{3,2,1,0:T(8,128)(2,1)S(1)}, bf16[1,6,32,256]{3,2,1,0:T(8,128)(2,1)S(1)}, u32[]{:S(2)}, u32[]{:S(2)}) collective-permute-start(bf16[1,6,32,256]{3,2,1,0:T(8,128)(2,1)S(1)} %constant_dynamic-update-slice_fusion), channel_id=1, source_target_pairs={{1,0},{2,1},{3,2},{4,3},{5,4},{6,5},{7,6},{8,7},{9,8},{10,9},{11,1... | collective-permute-start | bytes 294920 | tf_op jit(solution)/shard_map/ppermute | solution.py:19
  38.0 4.4 copy-start.297
  38.9 3.5 copy-start.298
  39.8 4.2 copy-start.468
  60.5 8.2 %copy-start.5 = (bf16[1,32,4096]{2,1,0:T(8,128)(2,1)}, bf16[1,32,4096]{2,1,0:T(8,128)(2,1)S(1)}, u32[]{:S(2)}) copy-start(bf16[1,32,4096]{2,1,0:T(8,128)(2,1)S(1)} %copy.608) | copy-start | bytes 786436
  117.9 3.1 copy-start.11
  117.9 3.1 copy-start.20
  136.1 7.7 %copy-start.24 = (bf16[1,9,32,4096]{3,2,1,0:T(8,128)(2,1)S(1)}, bf16[1,9,32,4096]{3,2,1,0:T(8,128)(2,1)}, u32[]{:S(2)}) copy-start(bf16[1,9,32,4096]{3,2,1,0:T(8,128)(2,1)} %copy-done.23) | copy-start | bytes 7077892
  138.6 47.3 %collective-permute-start.2 = (bf16[1,6,32,256]{3,2,1,0:T(8,128)(2,1)}, bf16[1,6,32,256]{3,2,1,0:T(8,128)(2,1)}, u32[]{:S(2)}, u32[]{:S(2)}) collective-permute-start(bf16[1,6,32,256]{3,2,1,0:T(8,128)(2,1)} %constant_dynamic-update-slice_fusion.33), channel_id=1, source_target_pairs={{255,0},{0,1},{1,2},{2,3},{3,4},{4,5},{5,6},{6,7},{7,8},{8,9},{9,1... | collective-permute-start | bytes 294920 | tf_op jit(solution)/shard_map/ppermute | solution.py:19
  138.6 47.3 %collective-permute-start.3 = (bf16[1,6,32,256]{3,2,1,0:T(8,128)(2,1)}, bf16[1,6,32,256]{3,2,1,0:T(8,128)(2,1)}, u32[]{:S(2)}, u32[]{:S(2)}) collective-permute-start(bf16[1,6,32,256]{3,2,1,0:T(8,128)(2,1)} %constant_dynamic-update-slice_fusion.33), channel_id=1, source_target_pairs={{1,0},{2,1},{3,2},{4,3},{5,4},{6,5},{7,6},{8,7},{9,8},{10,9},{11,1... | collective-permute-start | bytes 294920 | tf_op jit(solution)/shard_map/ppermute | solution.py:19
  153.7 33.8 %collective-permute-start.6 = (bf16[1,6,32,256]{3,2,1,0:T(8,128)(2,1)}, bf16[1,6,32,256]{3,2,1,0:T(8,128)(2,1)}, u32[]{:S(2)}, u32[]{:S(2)}) collective-permute-start(bf16[1,6,32,256]{3,2,1,0:T(8,128)(2,1)} %constant_dynamic-update-slice_fusion.99), channel_id=1, source_target_pairs={{255,0},{0,1},{1,2},{2,3},{3,4},{4,5},{5,6},{6,7},{7,8},{8,9},{9,1... | collective-permute-start | bytes 294920 | tf_op jit(solution)/shard_map/ppermute | solution.py:19
  153.7 33.8 %collective-permute-start.7 = (bf16[1,6,32,256]{3,2,1,0:T(8,128)(2,1)}, bf16[1,6,32,256]{3,2,1,0:T(8,128)(2,1)}, u32[]{:S(2)}, u32[]{:S(2)}) collective-permute-start(bf16[1,6,32,256]{3,2,1,0:T(8,128)(2,1)} %constant_dynamic-update-slice_fusion.99), channel_id=1, source_target_pairs={{1,0},{2,1},{3,2},{4,3},{5,4},{6,5},{7,6},{8,7},{9,8},{10,9},{11,1... | collective-permute-start | bytes 294920 | tf_op jit(solution)/shard_map/ppermute | solution.py:19
  177.8 3.5 copy-start.16
  179.6 3.6 copy-start.12
  197.4 4.4 copy-start.308
  219.7 20.5 %copy-start.3 = (bf16[1,32,4096]{2,1,0:T(8,128)(2,1)}, bf16[1,32,4096]{2,1,0:T(8,128)(2,1)S(1)}, u32[]{:S(2)}) copy-start(bf16[1,32,4096]{2,1,0:T(8,128)(2,1)S(1)} %copy.749) | copy-start | bytes 786436
  230.6 11.4 %copy-start.1 = (bf16[1,32,4096]{2,1,0:T(8,128)(2,1)}, bf16[1,32,4096]{2,1,0:T(8,128)(2,1)S(1)}, u32[]{:S(2)}) copy-start(bf16[1,32,4096]{2,1,0:T(8,128)(2,1)S(1)} %copy.755) | copy-start | bytes 786436
  261.0 3.1 copy-start.261
  272.1 3.3 copy-start.303
  (456 other events, 820.4 us)
Sparse Core Ops, SparseCore 0:
  273.1 268.5 all-reduce.298
where the time goes:
time: 559 us; the launch traced here: 552 us
  waiting for transfers between devices  260 us (47%)
  local copies, waits for them, and re-layouts  200 us (36%)
  other arithmetic  30 us (5%)
  matrix products  24.9 us (4%)
  between operations  24 us (4%)
  starting transfers between devices  13.8 us (2%)
    psum x1, waiting for transfers between devices, local(): lax.psum((partial_one, partial_two), ('blocks', 'section'))  260 us
    slice x148, local copies, waits for them, and re-layouts, sliding_flattened(): return jnp.concatenate([field[..., amount:], zeros_pad], axis=-1)  120 us
    unnamed x968, local copies, waits for them, and re-layouts  22.6 us
    unnamed x46, other arithmetic  21.9 us
    broadcast_in_dim x16, local copies, waits for them, and re-layouts, spread_rims(): spread_z = [jnp.repeat(rims[:, face], EDGE, axis=2) for face in (4, 5)]  16.8 us
    dot_general x12, matrix products, convolve(): jnp.einsum('cr,xrq->xcq', weight_matrix, stacked_tiles, preferred_element...  14.2 us
    ppermute x8, starting transfers between devices, from_behind(): return lax.ppermute(block, axis, route)  13.8 us
    another operation x16, local copies, waits for them, and re-layouts, spread_rims(): jnp.tile(rims[:, face].reshape(number, C, EDGE, EDGE), (1, 1, 1, EDGE))  12.8 us
  transfers between devices with their start and end apart: 9, of which 1 were waited for; matrix products, arithmetic and copies ran while one was open for 15% of the time, Pallas kernels for 0%

commit v1 on v0

v1 whole, which is shorter than its diff:
```python
import functools
import math

import jax
import jax.numpy as jnp
import numpy as np
from jax import lax
from jax.experimental import pallas as pl
from jax.experimental.pallas import tpu as pltpu
from jax.sharding import PartitionSpec as P

C = 32
EDGE = 16
PLANE = EDGE * EDGE
SLABS = EDGE + 2
KEEP = 1024.0 / 819.0
MESH = pl.DeviceIdType.MESH
BF = jnp.bfloat16
F32 = jnp.float32

SHIFTS = [s for s in range(9) if s != 4] + [4]
PLACE = {s: i for i, s in enumerate(SHIFTS)}


def shift_matrices():
    table = np.zeros((PLANE + 128, 8 * PLANE), np.float32)
    for i, s in enumerate(SHIFTS[:8]):
        dy, dz = s // 3 - 1, s % 3 - 1
        for y in range(EDGE):
            for z in range(EDGE):
                column = i * PLANE + y * EDGE + z
                sy, sz = y + dy, z + dz
                in_y, in_z = 0 <= sy < EDGE, 0 <= sz < EDGE
                if in_y and in_z:
                    table[sy * EDGE + sz, column] = 1
                elif in_z:
                    slot = 0 if sy < 0 else 1
                    for half in (0, 64):
                        table[PLANE + half + slot * EDGE + sz, column] = 1
                elif in_y:
                    slot = 2 if sz < 0 else 3
                    for half in (0, 64):
                        table[PLANE + half + slot * EDGE + sy, column] = 1
    return table


def face_matrix():
    table = np.zeros((2 * PLANE, 128), np.float32)
    for half in (0, 1):
        for i in range(EDGE):
            base = half * 64
            table[half * PLANE + (EDGE - 1) * EDGE + i, base + i] = 1
            table[half * PLANE + i, base + EDGE + i] = 1
            table[half * PLANE + i * EDGE + EDGE - 1, base + 2 * EDGE + i] = 1
            table[half * PLANE + i * EDGE, base + 3 * EDGE + i] = 1
    return table


def dot(a, b):
    return jnp.dot(a, b, preferred_element_type=F32)


def dot_nt(a, b):
    return lax.dot_general(a, b, (((1,), (1,)), ((), ())), preferred_element_type=F32)


def kernel(
    count,
    feat_ref,
    pool_ref,
    skip_ref,
    one_ref,
    two_ref,
    shift_ref,
    face_ref,
    links_ref,
    pos_ref,
    seed_ref,
    enc_ref,
    gfeat_ref,
    gone_ref,
    gtwo_ref,
    v_f,
    v_u,
    v_d,
    v_i,
    im_f,
    im_u,
    im_d,
    im_i,
    w_one,
    w_two,
    wt_one,
    wt_two,
    y_buf,
    z_buf,
    keep_buf,
    d_all,
    i_all,
    sendf,
    recvp,
    recvn,
    g_full,
    g_send,
    g_slots,
    z_slots,
    r_send,
    fin,
    fsend_sem,
    frecv_sem,
    s1_send,
    s1_recv,
    s2_send,
    s2_recv,
    s3_send,
    s3_recv,
):
    blocks, section = lax.axis_index("blocks"), lax.axis_index("section")
    per = lax.axis_size("section")
    me = blocks * per + section
    group = 32
    rings = count // group
    ring, rank = me // group, lax.rem(me, group)

    def at(index):
        return (index // per, lax.rem(index, per))

    nxt = lax.rem(me + 1, count)
    prv = lax.rem(me + count - 1, count)

    barrier = pltpu.get_barrier_semaphore()
    for d in (prv, nxt):
        pl.semaphore_signal(barrier, inc=1, device_id=at(d), device_id_type=MESH)

    def greet_group(o, carry):
        t = ring * group + lax.rem(rank + o, group)
        pl.semaphore_signal(barrier, inc=1, device_id=at(t), device_id_type=MESH)
        return carry

    lax.fori_loop(1, group, greet_group, 0)

    def greet_ring(o, carry):
        t = lax.rem(ring + o, rings) * group + rank
        pl.semaphore_signal(barrier, inc=1, device_id=at(t), device_id_type=MESH)
        return carry

    lax.fori_loop(1, rings, greet_ring, 0)

    for x in range(EDGE):
        rows, lanes = pl.ds((x + 1) * C, C), pl.ds(x * PLANE, PLANE)
        v_f[rows, 0:PLANE] = feat_ref[0, :, lanes]
        v_u[rows, 0:PLANE] = (
            pool_ref[0, :, lanes].astype(F32) + skip_ref[0, :, lanes].astype(F32)
        ).astype(BF)
    zero = jnp.zeros((C, 128), BF)
    for v in (v_f, v_u, v_d, v_i):
        v[0:C, PLANE:] = zero
        v[(SLABS - 1) * C :, PLANE:] = zero

    inner_rows = pl.ds(C, EDGE * C)

    def pack_faces(v, slot):
        last = EDGE * C
        sendf[slot, 0:32, :] = v[last : last + C, 0:128]
        sendf[slot, 32:64, :] = v[last : last + C, 128:256]
        sendf[slot, 64:96, :] = v[C : 2 * C, 0:128]
        sendf[slot, 96:128, :] = v[C : 2 * C, 128:256]
        packed = dot(v[C : 9 * C, 0:PLANE], face_ref[0:PLANE, :]) + dot(
            v[9 * C : 17 * C, 0:PLANE], face_ref[PLANE:, :]
        )
        sendf[slot, 128:384, :] = packed.astype(BF)

    def face_copies(slot):
        to_next = pltpu.make_async_remote_copy(
            src_ref=sendf.at[slot],
            dst_ref=recvp.at[slot],
            send_sem=fsend_sem.at[2 * slot],
            recv_sem=frecv_sem.at[2 * slot],
            device_id=at(nxt),
            device_id_type=MESH,
        )
        to_prev = pltpu.make_async_remote_copy(
            src_ref=sendf.at[slot],
            dst_ref=recvn.at[slot],
            send_sem=fsend_sem.at[2 * slot + 1],
            recv_sem=frecv_sem.at[2 * slot + 1],
            device_id=at(prv),
            device_id_type=MESH,
        )
        return to_next, to_prev

    def send_faces(slot):
        copies = face_copies(slot)
        for copy in copies:
            copy.start()
        return copies

    pack_faces(v_f, 0)
    pack_faces(v_u, 1)
    pl.semaphore_wait(barrier, 2 + (group - 1) + (rings - 1))
    sent = [send_faces(0), send_faces(1)]

    def weights(ref, plain, mirrored):
        for k in range(3):
            plain[k * C : (k + 1) * C, :] = jnp.concatenate(
                [ref[k * 9 + s].astype(F32) for s in SHIFTS], axis=1
            ).astype(BF)
        stacked = jnp.concatenate(
            [
                jnp.concatenate(
                    [ref[26 - (k * 9 + s)].astype(F32) for k in range(3)]
                    + [jnp.zeros((C, C), F32)],
                    axis=1,
                )
                for s in SHIFTS
            ]
            + [jnp.zeros((96, 128), F32)],
            axis=0,
        )
        mirrored[...] = jnp.transpose(stacked)[0:96, 0:288].astype(BF)

    weights(one_ref, w_one, wt_one)
    weights(two_ref, w_two, wt_two)

    lane = lax.broadcasted_iota(jnp.int32, (C, PLANE), 1)
    channel = lax.broadcasted_iota(jnp.int32, (C, PLANE), 0)
    base = (pos_ref[0, 1] * EDGE + lax.shift_right_logical(lane, 4)) * jnp.int32(19349663)
    base = base ^ ((pos_ref[0, 2] * EDGE + (lane & 15)) * jnp.int32(83492791))
    base = base ^ (channel * jnp.int32(1103515245))
    base = base ^ (seed_ref[0] * jnp.int32(668265263))
    for x in range(EDGE):
        h = base ^ ((pos_ref[0, 0] * EDGE + x) * jnp.int32(73856093))
        h = h ^ lax.shift_right_logical(h, 13)
        h = h * jnp.int32(1274126177)
        h = h ^ lax.shift_right_logical(h, 16)
        keep_buf[x * C : (x + 1) * C, :] = jnp.where((h & 1023) >= 205, F32(KEEP), F32(0.0))

    for k in range(3):
        for j in range(SLABS):
            if not 0 <= j - k < EDGE:
                for ref in (d_all, i_all):
                    ref[k * C : (k + 1) * C, j * PLANE : (j + 1) * PLANE] = jnp.zeros(
                        (C, PLANE), BF
                    )

    def shift_here(v, im):
        for x in range(EDGE):
            im[8 * C :, (x + 1) * PLANE : (x + 2) * PLANE] = v[(x + 1) * C : (x + 2) * C, 0:PLANE]
        for i in range(8):
            moved = dot(v[inner_rows, 0:PLANE], shift_ref[0:PLANE, i * PLANE : (i + 1) * PLANE])
            for x in range(EDGE):
                im[i * C : (i + 1) * C, (x + 1) * PLANE : (x + 2) * PLANE] = moved[
                    x * C : (x + 1) * C
                ].astype(BF)

    shift_here(v_f, im_f)
    shift_here(v_u, im_u)

    mlane = lax.broadcasted_iota(jnp.int32, (16, 128), 1)
    slot_of = lax.shift_right_logical(mlane, 4) & 3
    wanted = jnp.full((16, 128), -1, jnp.int32)
    for k in range(4):
        wanted = jnp.where(slot_of == k, links_ref[0, 2 + k], wanted)

    def weight_of(condition):
        return jnp.where(condition, F32(1.0), F32(0.0)).astype(BF)[0:1, :]

    low = mlane < 64
    p_low = weight_of((wanted == prv) & low)
    n_low = weight_of((wanted == nxt) & low)
    p_high = weight_of((wanted == prv) & (mlane >= 64))
    n_high = weight_of((wanted == nxt) & (mlane >= 64))
    x_masks = []
    for k in range(2):
        link = jnp.full((16, 128), links_ref[0, k], jnp.int32)
        x_masks.append((weight_of(link == prv), weight_of(link == nxt)))

    def take_rims(v, im, slot):
        for k in range(2):
            mp, mn = x_masks[k]
            row = 0 if k == 0 else (SLABS - 1) * C
            for half in range(2):
                at_rows = pl.ds(k * 64 + half * 32, 32)
                v[row : row + C, half * 128 : half * 128 + 128] = (
                    recvp[slot, at_rows, :] * mp + recvn[slot, at_rows, :] * mn
                )
        from_p, from_n = recvp[slot, 128:384, :], recvn[slot, 128:384, :]
        v[C : 9 * C, PLANE:] = from_p * p_low + from_n * n_low
        v[9 * C : 17 * C, PLANE:] = from_p * p_high + from_n * n_high
        for j in (0, SLABS - 1):
            rows, lanes = pl.ds(j * C, C), pl.ds(j * PLANE, PLANE)
            im[8 * C :, lanes] = v[rows, 0:PLANE]
        for i in range(8):
            rim = dot(v[inner_rows, PLANE:], shift_ref[PLANE:, i * PLANE : (i + 1) * PLANE])
            for x in range(EDGE):
                rows, lanes = pl.ds(i * C, C), pl.ds((x + 1) * PLANE, PLANE)
                im[rows, lanes] = im[rows, lanes] + rim[x * C : (x + 1) * C].astype(BF)
            for j in (0, SLABS - 1):
                im[i * C : (i + 1) * C, j * PLANE : (j + 1) * PLANE] = dot(
                    v[j * C : (j + 1) * C, 0:PLANE], shift_ref[0:PLANE, i * PLANE : (i + 1) * PLANE]
                ).astype(BF)

    def convolve(w, im, out):
        for j in range(0, SLABS, 2):
            lanes = pl.ds(j * PLANE, 2 * PLANE)
            out[:, lanes] = dot(w[...], im[:, lanes])

    def summed(y, x):
        return (
            y[0:C, x * PLANE : (x + 1) * PLANE]
            + y[C : 2 * C, (x + 1) * PLANE : (x + 2) * PLANE]
            + y[2 * C : 3 * C, (x + 2) * PLANE : (x + 3) * PLANE]
        )

    def arrive(slot):
        for copy in sent[slot]:
            copy.wait_recv()

    arrive(0)
    take_rims(v_f, im_f, 0)
    convolve(w_one, im_f, y_buf)
    for x in range(EDGE):
        pre = summed(y_buf, x)
        value = (jax.nn.silu(pre) * keep_buf[x * C : (x + 1) * C, :]).astype(BF)
        v_d[(x + 1) * C : (x + 2) * C, 0:PLANE] = value
        for k in range(3):
            d_all[k * C : (k + 1) * C, (x + k) * PLANE : (x + k + 1) * PLANE] = value
    pack_faces(v_d, 2)
    sent.append(send_faces(2))

    arrive(1)
    take_rims(v_u, im_u, 1)
    convolve(wt_two, im_u, z_buf)
    for x in range(EDGE):
        pre = summed(y_buf, x)
        back = summed(z_buf, x)
        logistic = jax.nn.sigmoid(pre)
        keep = keep_buf[x * C : (x + 1) * C, :]
        value = (back * keep * logistic * (1.0 + pre * (1.0 - logistic))).astype(BF)
        v_i[(x + 1) * C : (x + 2) * C, 0:PLANE] = value
        for k in range(3):
            i_all[k * C : (k + 1) * C, (x + k) * PLANE : (x + k + 1) * PLANE] = value
    pack_faces(v_i, 3)
    sent.append(send_faces(3))

    g_two = dot_nt(im_u[...], d_all[...])
    g_full[0:288, 0:96] = g_two
    g_full[0:288, 96:128] = jnp.zeros((288, 32), F32)
    g_one = dot_nt(i_all[...], im_f[...])
    g_full[288:384, :] = g_one[:, 0:128]
    g_full[384:480, :] = g_one[:, 128:256]
    g_full[480:512, :] = jnp.concatenate(
        [g_one[k * C : (k + 1) * C, 256:288] for k in range(3)] + [jnp.zeros((C, C), F32)], axis=1
    )
    g_send[...] = g_full[...].astype(BF)

    def chunk(index):
        return pl.ds(pl.multiple_of(index * 16, 16), 16)

    def scatter_copy(o):
        t = lax.rem(rank + o, group)
        return pltpu.make_async_remote_copy(
            src_ref=g_send.at[chunk(t), :],
            dst_ref=g_slots.at[o],
            send_sem=s1_send.at[o],
            recv_sem=s1_recv.at[o],
            device_id=at(ring * group + t),
            device_id_type=MESH,
        )

    def ring_copy(o):
        t = lax.rem(ring + o, rings)
        return pltpu.make_async_remote_copy(
            src_ref=z_slots.at[ring],
            dst_ref=z_slots.at[ring],
            send_sem=s2_send.at[o],
            recv_sem=s2_recv.at[o],
            device_id=at(t * group + rank),
            device_id_type=MESH,
        )

    def gather_copy(o):
        t = lax.rem(rank + o, group)
        return pltpu.make_async_remote_copy(
            src_ref=r_send,
            dst_ref=fin.at[chunk(rank), :],
            send_sem=s3_send.at[o],
            recv_sem=s3_recv.at[o],
            device_id=at(ring * group + t),
            device_id_type=MESH,
        )

    def each(copy_of, upto, act):
        def step(o, carry):
            act(copy_of(o))
            return carry

        lax.fori_loop(1, upto, step, 0)

    each(scatter_copy, group, lambda c: c.start())

    shift_here(v_d, im_d)

    each(scatter_copy, group, lambda c: c.wait_recv())
    total = g_full[chunk(rank), :]
    for o in range(1, group):
        total = total + g_slots[o].astype(F32)
    z_slots[ring] = total
    each(ring_copy, rings, lambda c: c.start())

    shift_here(v_i, im_i)

    arrive(2)
    take_rims(v_d, im_d, 2)
    convolve(w_two, im_d, y_buf)
    for x in range(EDGE):
        enc_ref[0, :, x * PLANE : (x + 1) * PLANE] = summed(y_buf, x).astype(BF)

    each(ring_copy, rings, lambda c: c.wait_recv())
    total = z_slots[0]
    for o in range(1, rings):
        total = total + z_slots[o]
    r_send[...] = total.astype(BF)
    fin[chunk(rank), :] = total.astype(BF)
    each(gather_copy, group, lambda c: c.start())

    arrive(3)
    take_rims(v_i, im_i, 3)
    convolve(wt_one, im_i, z_buf)
    for x in range(EDGE):
        gfeat_ref[0, :, x * PLANE : (x + 1) * PLANE] = summed(z_buf, x).astype(BF)

    each(gather_copy, group, lambda c: c.wait_recv())
    norm = F32(1.0 / math.sqrt(count * EDGE**3))
    for k in range(3):
        for s in range(9):
            p, q = PLACE[s], PLACE[8 - s]
            if p < 8:
                top, left = 288 + 96 * (p // 4) + k * C, (p % 4) * C
            else:
                top, left = 480, k * C
            rows = fin[top : top + C, :].astype(F32)
            gone_ref[k * 9 + s] = rows[:, left : left + C] * norm
            rows = fin[q * C : (q + 1) * C, :].astype(F32)
            gtwo_ref[k * 9 + s] = rows[:, (2 - k) * C : (3 - k) * C] * norm

    for pair in sent:
        for copy in pair:
            copy.wait_send()
    each(scatter_copy, group, lambda c: c.wait_send())
    each(ring_copy, rings, lambda c: c.wait_send())
    each(gather_copy, group, lambda c: c.wait_send())


def local(count, *args):
    features, pool, skip, one, two, links, positions, seed = args
    shift = jnp.asarray(shift_matrices(), BF)
    face = jnp.asarray(face_matrix(), BF)
    vmem = pl.BlockSpec(memory_space=pltpu.VMEM)
    smem = pl.BlockSpec(memory_space=pltpu.SMEM)
    rows, lanes = SLABS * C, SLABS * PLANE
    dma = pltpu.SemaphoreType.DMA
    rings = count // 32
    return pl.pallas_call(
        functools.partial(kernel, count),
        out_shape=(
            jax.ShapeDtypeStruct((1, C, EDGE**3), BF),
            jax.ShapeDtypeStruct((1, C, EDGE**3), BF),
            jax.ShapeDtypeStruct((27, C, C), F32),
            jax.ShapeDtypeStruct((27, C, C), F32),
        ),
        in_specs=[vmem] * 7 + [smem] * 3,
        out_specs=(vmem,) * 4,
        scratch_shapes=[pltpu.VMEM((rows, PLANE + 128), BF)] * 4
        + [pltpu.VMEM((9 * C, lanes), BF)] * 4
        + [pltpu.VMEM((96, 288), BF)] * 4
        + [pltpu.VMEM((96, lanes), F32)] * 2
        + [pltpu.VMEM((EDGE * C, PLANE), F32)]
        + [pltpu.VMEM((96, lanes), BF)] * 2
        + [pltpu.VMEM((4, 384, 128), BF)] * 3
        + [
            pltpu.VMEM((512, 128), F32),
            pltpu.VMEM((512, 128), BF),
            pltpu.VMEM((32, 16, 128), BF),
            pltpu.VMEM((rings, 16, 128), F32),
            pltpu.VMEM((16, 128), BF),
            pltpu.VMEM((512, 128), BF),
            dma((8,)),
            dma((8,)),
            dma((32,)),
            dma((32,)),
            dma((rings,)),
            dma((rings,)),
            dma((32,)),
            dma((32,)),
        ],
        compiler_params=pltpu.CompilerParams(
            collective_id=0, has_side_effects=True, vmem_limit_bytes=48 * 2**20
        ),
        cost_estimate=pl.CostEstimate(
            flops=4_000_000_000, bytes_accessed=3_000_000, transcendentals=300_000
        ),
    )(features, pool, skip, one, two, shift, face, links, positions, seed)


def solution(mesh):
    both = ("blocks", "section")
    in_specs = (
        P(both, None, None),
        P(both, None, None),
        P(both, None, None),
        P(),
        P(),
        P(both, None),
        P(both, None),
        P(),
    )
    out_specs = (P(both, None, None), P(both, None, None), P(), P())
    return jax.shard_map(
        functools.partial(local, mesh.size),
        mesh=mesh,
        in_specs=in_specs,
        out_specs=out_specs,
        check_vma=False,
    )
```

time: 559 us -> 53.7 us (0.10); the launches traced: 552 us -> 53.4 us
  waiting for transfers between devices: 260 us -> 0 us
  local copies, waits for them, and re-layouts: 200 us -> 11.3 us
  Pallas kernels: 0 us -> 40.8 us
  other arithmetic: 30 us -> 0 us
  matrix products: 24.9 us -> 0 us
  between operations: 24 us -> 1.31 us
  starting transfers between devices: 13.8 us -> 0 us
    psum x1 -> x0, waiting for transfers between devices: 260 us -> none  [local(): lax.psum((partial_one, partial_two), ('blocks', 'section'))]
    slice x171 -> x0, local copies, waits for them, and re-layouts: 129 us -> none  [the longest x148 120 us: sliding_flattened(): return jnp.concatenate([field[..., amount:], zeros_pad], axis=-1)]
    pallas_call x0 -> x1, Pallas kernels: none -> 40.8 us  [local(): pl.pallas_call(functools.partial(kernel, count), out_shape=(jax.ShapeDtyp...]
    dot_general x18 -> x0, matrix products: 24.9 us -> none  [the longest x12 14.2 us: convolve(): jnp.einsum('cr,xrq->xcq', weight_matrix, stacked_tiles, preferred_element...]
    unnamed x46 -> x0, other arithmetic: 21.9 us -> none
    another operation x47 -> x0, local copies, waits for them, and re-layouts: 19.7 us -> none  [the longest x16 12.8 us: spread_rims(): jnp.tile(rims[:, face].reshape(number, C, EDGE, EDGE), (1, 1, 1, EDGE))]
    broadcast_in_dim x16 -> x0, local copies, waits for them, and re-layouts: 16.8 us -> none  [spread_rims(): spread_z = [jnp.repeat(rims[:, face], EDGE, axis=2) for face in (4, 5)]]
    ppermute x8 -> x0, starting transfers between devices: 13.8 us -> none  [from_behind(): return lax.ppermute(block, axis, route)]
  transfers between devices with their start and end apart: 9 -> 0, of which waited for: 1 -> 0; matrix products, arithmetic and copies ran while one was open for 15% -> 0% of each run, Pallas kernels for 0% -> 0%
where the time goes in v1:
time: 53.7 us; the launch traced here: 53.4 us
  Pallas kernels  40.8 us (76%)
  local copies, waits for them, and re-layouts  11.3 us (21%)
  between operations  1.31 us (2%)
    pallas_call x1, Pallas kernels, local(): pl.pallas_call(functools.partial(kernel, count), out_shape=(jax.ShapeDtyp...  40.8 us
    unnamed x22, local copies, waits for them, and re-layouts  11.3 us

profile of v1, /device:TPU:1, one launch (start us, length us, event | category | flops | bytes accessed | tf_op | source)
XLA Modules:
  0.0 53.4 jit_solution(11260036496849617666)
XLA Ops:
  1.3 0.0 copy-start
  1.3 0.9 %copy-done = bf16[1,32,4096]{2,1,0:T(8,128)(2,1)S(1)} copy-done((bf16[1,32,4096]{2,1,0:T(8,128)(2,1)S(1)}, bf16[1,32,4096]{2,1,0:T(8,128)(2,1)}, u32[]{:S(2)}) %copy-start) | copy-done | bytes 262168
  2.2 0.0 copy-start.1
  2.2 0.9 %copy-done.1 = bf16[1,32,4096]{2,1,0:T(8,128)(2,1)S(1)} copy-done((bf16[1,32,4096]{2,1,0:T(8,128)(2,1)S(1)}, bf16[1,32,4096]{2,1,0:T(8,128)(2,1)}, u32[]{:S(2)}) %copy-start.1) | copy-done | bytes 262168
  3.2 0.0 copy-start.2
  3.2 0.9 %copy-done.2 = bf16[1,32,4096]{2,1,0:T(8,128)(2,1)S(1)} copy-done((bf16[1,32,4096]{2,1,0:T(8,128)(2,1)S(1)}, bf16[1,32,4096]{2,1,0:T(8,128)(2,1)}, u32[]{:S(2)}) %copy-start.2) | copy-done | bytes 262168
  4.1 0.0 copy-start.3
  4.1 0.9 %copy-done.3 = bf16[27,32,32]{2,1,0:T(8,128)(2,1)S(1)} copy-done((bf16[27,32,32]{2,1,0:T(8,128)(2,1)S(1)}, bf16[27,32,32]{2,1,0:T(8,128)(2,1)}, u32[]{:S(2)}) %copy-start.3) | copy-done | bytes 55320
  5.1 0.0 copy-start.4
  5.1 0.9 %copy-done.4 = bf16[27,32,32]{2,1,0:T(8,128)(2,1)S(1)} copy-done((bf16[27,32,32]{2,1,0:T(8,128)(2,1)S(1)}, bf16[27,32,32]{2,1,0:T(8,128)(2,1)}, u32[]{:S(2)}) %copy-start.4) | copy-done | bytes 55320
  6.0 0.0 copy-start.5
  6.0 0.7 %copy-done.5 = s32[1,6]{1,0:T(1,128)S(1)} copy-done((s32[1,6]{1,0:T(1,128)S(1)}, s32[1,6]{1,0:T(1,128)}, u32[]{:S(2)}) %copy-start.5) | copy-done | bytes 48
  6.7 0.0 copy-start.6
  6.7 0.7 %copy-done.6 = s32[1,3]{1,0:T(1,128)S(1)} copy-done((s32[1,3]{1,0:T(1,128)S(1)}, s32[1,3]{1,0:T(1,128)}, u32[]{:S(2)}) %copy-start.6) | copy-done | bytes 36
  7.3 0.0 copy-start.7
  7.3 1.4 %copy-done.7 = bf16[384,2048]{1,0:T(8,128)(2,1)S(1)} copy-done((bf16[384,2048]{1,0:T(8,128)(2,1)S(1)}, bf16[384,2048]{1,0:T(8,128)(2,1)}, u32[]{:S(2)}) %copy-start.7) | copy-done | bytes 1572888
  8.7 0.0 copy-start.8
  8.7 0.9 %copy-done.8 = bf16[512,128]{1,0:T(8,128)(2,1)S(1)} copy-done((bf16[512,128]{1,0:T(8,128)(2,1)S(1)}, bf16[512,128]{1,0:T(8,128)(2,1)}, u32[]{:S(2)}) %copy-start.8) | copy-done | bytes 131096
  9.6 40.8 %shard_map.129 = (bf16[1,32,4096]{2,1,0:T(8,128)(2,1)S(1)}, bf16[1,32,4096]{2,1,0:T(8,128)(2,1)S(1)}, f32[27,32,32]{2,1,0:T(8,128)S(1)}, f32[27,32,32]{2,1,0:T(8,128)S(1)}) custom-call(bf16[1,32,4096]{2,1,0:T(8,128)(2,1)S(1)} %copy-done, bf16[1,32,4096]{2,1,0:T(8,128)(2,1)S(1)} %copy-done.1, bf16[1,32,4096]{2,1,0:T(8,128)(2,1)S(1)} %copy-done.2, ...), custom_call_target="tpu_custom_call" | custom-call | flops 4000000000 | bytes 3000000 | tf_op jit(solution)/shard_map/pallas_call | solution.py:464
  50.4 0.7 %copy.19 = bf16[1,32,4096]{2,1,0:T(8,128)(2,1)} copy(bf16[1,32,4096]{2,1,0:T(8,128)(2,1)S(1)} %get-tuple-element.8) | data formatting | bytes 524288
  51.1 0.7 %copy.20 = bf16[1,32,4096]{2,1,0:T(8,128)(2,1)} copy(bf16[1,32,4096]{2,1,0:T(8,128)(2,1)S(1)} %get-tuple-element.9) | data formatting | bytes 524288
  51.9 0.8 %copy.21 = f32[27,32,32]{2,1,0:T(8,128)} copy(f32[27,32,32]{2,1,0:T(8,128)S(1)} %get-tuple-element.10) | data formatting | bytes 221184
  52.6 0.8 %copy.22 = f32[27,32,32]{2,1,0:T(8,128)} copy(f32[27,32,32]{2,1,0:T(8,128)S(1)} %get-tuple-element.11) | data formatting | bytes 221184
Async XLA Ops:
  1.3 1.0 %copy-start = (bf16[1,32,4096]{2,1,0:T(8,128)(2,1)S(1)}, bf16[1,32,4096]{2,1,0:T(8,128)(2,1)}, u32[]{:S(2)}) copy-start(bf16[1,32,4096]{2,1,0:T(8,128)(2,1)} %feat_ref.1) | copy-start | bytes 786436
  2.2 0.9 %copy-start.1 = (bf16[1,32,4096]{2,1,0:T(8,128)(2,1)S(1)}, bf16[1,32,4096]{2,1,0:T(8,128)(2,1)}, u32[]{:S(2)}) copy-start(bf16[1,32,4096]{2,1,0:T(8,128)(2,1)} %pool_ref.1) | copy-start | bytes 786436
  3.2 0.9 %copy-start.2 = (bf16[1,32,4096]{2,1,0:T(8,128)(2,1)S(1)}, bf16[1,32,4096]{2,1,0:T(8,128)(2,1)}, u32[]{:S(2)}) copy-start(bf16[1,32,4096]{2,1,0:T(8,128)(2,1)} %skip_ref.1) | copy-start | bytes 786436
  4.1 0.9 %copy-start.3 = (bf16[27,32,32]{2,1,0:T(8,128)(2,1)S(1)}, bf16[27,32,32]{2,1,0:T(8,128)(2,1)}, u32[]{:S(2)}) copy-start(bf16[27,32,32]{2,1,0:T(8,128)(2,1)} %one_ref.1) | copy-start | bytes 165892
  5.1 0.9 %copy-start.4 = (bf16[27,32,32]{2,1,0:T(8,128)(2,1)S(1)}, bf16[27,32,32]{2,1,0:T(8,128)(2,1)}, u32[]{:S(2)}) copy-start(bf16[27,32,32]{2,1,0:T(8,128)(2,1)} %two_ref.1) | copy-start | bytes 165892
  6.0 0.7 %copy-start.5 = (s32[1,6]{1,0:T(1,128)S(1)}, s32[1,6]{1,0:T(1,128)}, u32[]{:S(2)}) copy-start(s32[1,6]{1,0:T(1,128)} %links_ref.1) | copy-start | bytes 76
  6.7 0.7 %copy-start.6 = (s32[1,3]{1,0:T(1,128)S(1)}, s32[1,3]{1,0:T(1,128)}, u32[]{:S(2)}) copy-start(s32[1,3]{1,0:T(1,128)} %pos_ref.1) | copy-start | bytes 40
  7.3 1.4 %copy-start.7 = (bf16[384,2048]{1,0:T(8,128)(2,1)S(1)}, bf16[384,2048]{1,0:T(8,128)(2,1)}, u32[]{:S(2)}) copy-start(bf16[384,2048]{1,0:T(8,128)(2,1)} %constant.4.clone.shift_ref) | copy-start | bytes 4718596
  8.7 0.9 %copy-start.8 = (bf16[512,128]{1,0:T(8,128)(2,1)S(1)}, bf16[512,128]{1,0:T(8,128)(2,1)}, u32[]{:S(2)}) copy-start(bf16[512,128]{1,0:T(8,128)(2,1)} %constant.5.clone.face_ref) | copy-start | bytes 393220

commit v2 on v1

--- a/solution.py
+++ b/solution.py
@@ -66,6 +66,21 @@
 
 def kernel(
     count,
+    feat_hbm,
+    pool_hbm,
+    skip_hbm,
+    one_hbm,
+    two_hbm,
+    shift_hbm,
+    face_hbm,
+    links_hbm,
+    pos_hbm,
+    seed_hbm,
+    enc_hbm,
+    gfeat_hbm,
+    fin_hbm,
+    enc_ref,
+    gfeat_ref,
     feat_ref,
     pool_ref,
     skip_ref,
@@ -76,10 +91,6 @@
     links_ref,
     pos_ref,
     seed_ref,
-    enc_ref,
-    gfeat_ref,
-    gone_ref,
-    gtwo_ref,
     v_f,
     v_u,
     v_d,
@@ -92,9 +103,14 @@
     w_two,
     wt_one,
     wt_two,
+    c_one,
+    c_two,
+    ct_one,
+    ct_two,
     y_buf,
     z_buf,
     keep_buf,
+    pre_buf,
     d_all,
     i_all,
     sendf,
@@ -106,6 +122,8 @@
     z_slots,
     r_send,
     fin,
+    in_sem,
+    out_sem,
     fsend_sem,
     frecv_sem,
     s1_send,
@@ -128,27 +146,43 @@
     nxt = lax.rem(me + 1, count)
     prv = lax.rem(me + count - 1, count)
 
+    loads = {}
+    for i, (name, src, dst) in enumerate(
+        [
+            ("feat", feat_hbm, feat_ref),
+            ("face", face_hbm, face_ref),
+            ("pool", pool_hbm, pool_ref),
+            ("skip", skip_hbm, skip_ref),
+            ("shift", shift_hbm, shift_ref),
+            ("one", one_hbm, one_ref),
+            ("two", two_hbm, two_ref),
+            ("links", links_hbm, links_ref),
+            ("pos", pos_hbm, pos_ref),
+            ("seed", seed_hbm, seed_ref),
+        ]
+    ):
+        loads[name] = pltpu.make_async_copy(src, dst, in_sem.at[i])
+        loads[name].start()
+
     barrier = pltpu.get_barrier_semaphore()
     for d in (prv, nxt):
         pl.semaphore_signal(barrier, inc=1, device_id=at(d), device_id_type=MESH)
 
-    def greet_group(o, carry):
+    for o in range(1, group):
         t = ring * group + lax.rem(rank + o, group)
         pl.semaphore_signal(barrier, inc=1, device_id=at(t), device_id_type=MESH)
-        return carry
-
-    lax.fori_loop(1, group, greet_group, 0)
-
-    def greet_ring(o, carry):
+    for o in range(1, rings):
         t = lax.rem(ring + o, rings) * group + rank
         pl.semaphore_signal(barrier, inc=1, device_id=at(t), device_id_type=MESH)
-        return carry
-
-    lax.fori_loop(1, rings, greet_ring, 0)
-
+
+    loads["feat"].wait()
     for x in range(EDGE):
         rows, lanes = pl.ds((x + 1) * C, C), pl.ds(x * PLANE, PLANE)
         v_f[rows, 0:PLANE] = feat_ref[0, :, lanes]
+    loads["pool"].wait()
+    loads["skip"].wait()
+    for x in range(EDGE):
+        rows, lanes = pl.ds((x + 1) * C, C), pl.ds(x * PLANE, PLANE)
         v_u[rows, 0:PLANE] = (
             pool_ref[0, :, lanes].astype(F32) + skip_ref[0, :, lanes].astype(F32)
         ).astype(BF)
@@ -195,16 +229,23 @@
             copy.start()
         return copies
 
+    loads["face"].wait()
     pack_faces(v_f, 0)
     pack_faces(v_u, 1)
     pl.semaphore_wait(barrier, 2 + (group - 1) + (rings - 1))
     sent = [send_faces(0), send_faces(1)]
 
-    def weights(ref, plain, mirrored):
+    for name in ("one", "two", "links", "pos", "seed", "shift"):
+        loads[name].wait()
+
+    def weights(ref, plain, mirrored, centre, mirrored_centre):
         for k in range(3):
             plain[k * C : (k + 1) * C, :] = jnp.concatenate(
-                [ref[k * 9 + s].astype(F32) for s in SHIFTS], axis=1
+                [ref[k * 9 + s].astype(F32) for s in SHIFTS[:8]], axis=1
             ).astype(BF)
+        centre[...] = jnp.concatenate(
+            [ref[k * 9 + 4].astype(F32) for k in range(3)], axis=1
+        ).astype(BF)
         stacked = jnp.concatenate(
             [
                 jnp.concatenate(
@@ -217,10 +258,14 @@
             + [jnp.zeros((96, 128), F32)],
             axis=0,
         )
-        mirrored[...] = jnp.transpose(stacked)[0:96, 0:288].astype(BF)
-
-    weights(one_ref, w_one, wt_one)
-    weights(two_ref, w_two, wt_two)
+        turned = jnp.transpose(stacked)
+        mirrored[...] = turned[0:96, 0:256].astype(BF)
+        mirrored_centre[...] = jnp.concatenate(
+            [turned[k * C : (k + 1) * C, 256:288] for k in range(3)], axis=1
+        ).astype(BF)
+
+    weights(one_ref, w_one, wt_one, c_one, ct_one)
+    weights(two_ref, w_two, wt_two, c_two, ct_two)
 
     lane = lax.broadcasted_iota(jnp.int32, (C, PLANE), 1)
     channel = lax.broadcasted_iota(jnp.int32, (C, PLANE), 0)
@@ -244,8 +289,6 @@
                     )
 
     def shift_here(v, im):
-        for x in range(EDGE):
-            im[8 * C :, (x + 1) * PLANE : (x + 2) * PLANE] = v[(x + 1) * C : (x + 2) * C, 0:PLANE]
         for i in range(8):
             moved = dot(v[inner_rows, 0:PLANE], shift_ref[0:PLANE, i * PLANE : (i + 1) * PLANE])
             for x in range(EDGE):
@@ -287,27 +330,25 @@
         from_p, from_n = recvp[slot, 128:384, :], recvn[slot, 128:384, :]
         v[C : 9 * C, PLANE:] = from_p * p_low + from_n * n_low
         v[9 * C : 17 * C, PLANE:] = from_p * p_high + from_n * n_high
-        for j in (0, SLABS - 1):
-            rows, lanes = pl.ds(j * C, C), pl.ds(j * PLANE, PLANE)
-            im[8 * C :, lanes] = v[rows, 0:PLANE]
+        outer = jnp.concatenate([v[0:C, 0:PLANE], v[(SLABS - 1) * C :, 0:PLANE]], axis=0)
         for i in range(8):
             rim = dot(v[inner_rows, PLANE:], shift_ref[PLANE:, i * PLANE : (i + 1) * PLANE])
             for x in range(EDGE):
                 rows, lanes = pl.ds(i * C, C), pl.ds((x + 1) * PLANE, PLANE)
                 im[rows, lanes] = im[rows, lanes] + rim[x * C : (x + 1) * C].astype(BF)
-            for j in (0, SLABS - 1):
-                im[i * C : (i + 1) * C, j * PLANE : (j + 1) * PLANE] = dot(
-                    v[j * C : (j + 1) * C, 0:PLANE], shift_ref[0:PLANE, i * PLANE : (i + 1) * PLANE]
-                ).astype(BF)
+            ends = dot(outer, shift_ref[0:PLANE, i * PLANE : (i + 1) * PLANE]).astype(BF)
+            im[i * C : (i + 1) * C, 0:PLANE] = ends[0:C]
+            im[i * C : (i + 1) * C, (SLABS - 1) * PLANE :] = ends[C : 2 * C]
 
     def convolve(w, im, out):
         for j in range(0, SLABS, 2):
             lanes = pl.ds(j * PLANE, 2 * PLANE)
             out[:, lanes] = dot(w[...], im[:, lanes])
 
-    def summed(y, x):
+    def summed(y, x, centre, v):
         return (
-            y[0:C, x * PLANE : (x + 1) * PLANE]
+            dot(centre[...], v[x * C : (x + 3) * C, 0:PLANE])
+            + y[0:C, x * PLANE : (x + 1) * PLANE]
             + y[C : 2 * C, (x + 1) * PLANE : (x + 2) * PLANE]
             + y[2 * C : 3 * C, (x + 2) * PLANE : (x + 3) * PLANE]
         )
@@ -315,12 +356,63 @@
     def arrive(slot):
         for copy in sent[slot]:
             copy.wait_recv()
+
+    def chunk(index):
+        return pl.ds(pl.multiple_of(index * 16, 16), 16)
+
+    def scatter_copy(o):
+        t = lax.rem(rank + o, group)
+        return pltpu.make_async_remote_copy(
+            src_ref=g_send.at[chunk(t), :],
+            dst_ref=g_slots.at[o],
+            send_sem=s1_send.at[0],
+            recv_sem=s1_recv.at[0],
+            device_id=at(ring * group + t),
+            device_id_type=MESH,
+        )
+
+    def ring_copy(o):
+        t = lax.rem(ring + o, rings)
+        return pltpu.make_async_remote_copy(
+            src_ref=z_slots.at[ring],
+            dst_ref=z_slots.at[ring],
+            send_sem=s2_send.at[0],
+            recv_sem=s2_recv.at[0],
+            device_id=at(t * group + rank),
+            device_id_type=MESH,
+        )
+
+    def gather_copy(o):
+        t = lax.rem(rank + o, group)
+        return pltpu.make_async_remote_copy(
+            src_ref=r_send,
+            dst_ref=fin.at[chunk(rank), :],
+            send_sem=s3_send.at[0],
+            recv_sem=s3_recv.at[0],
+            device_id=at(ring * group + t),
+            device_id_type=MESH,
+        )
+
+    def all_of(slots, send_sem, recv_sem):
+        return pltpu.make_async_remote_copy(
+            src_ref=slots,
+            dst_ref=slots,
+            send_sem=send_sem.at[0],
+            recv_sem=recv_sem.at[0],
+            device_id=at(nxt),
+            device_id_type=MESH,
+        )
+
+    scattered = all_of(g_slots.at[pl.ds(1, group - 1)], s1_send, s1_recv)
+    ringed = all_of(z_slots.at[pl.ds(1, rings - 1)], s2_send, s2_recv)
+    gathered = all_of(g_slots.at[pl.ds(1, group - 1)], s3_send, s3_recv)
 
     arrive(0)
     take_rims(v_f, im_f, 0)
     convolve(w_one, im_f, y_buf)
     for x in range(EDGE):
-        pre = summed(y_buf, x)
+        pre = summed(y_buf, x, c_one, v_f)
+        pre_buf[x * C : (x + 1) * C, :] = pre
         value = (jax.nn.silu(pre) * keep_buf[x * C : (x + 1) * C, :]).astype(BF)
         v_d[(x + 1) * C : (x + 2) * C, 0:PLANE] = value
         for k in range(3):
@@ -330,107 +422,121 @@
 
     arrive(1)
     take_rims(v_u, im_u, 1)
+
+    g_two = dot_nt(d_all[...], im_u[...])
+    g_full[0:256, :] = jnp.transpose(jnp.concatenate([g_two, jnp.zeros((C, 256), F32)], axis=0))
+    centre = dot_nt(v_u[0:C, 0:PLANE], d_all[:, 0:PLANE])
+    for j in range(1, SLABS):
+        centre = centre + dot_nt(
+            v_u[j * C : (j + 1) * C, 0:PLANE], d_all[:, j * PLANE : (j + 1) * PLANE]
+        )
+    g_full[256:288, :] = jnp.concatenate([centre, jnp.zeros((C, C), F32)], axis=1)
+    g_send[0:288, :] = g_full[0:288, :].astype(BF)
+
     convolve(wt_two, im_u, z_buf)
     for x in range(EDGE):
-        pre = summed(y_buf, x)
-        back = summed(z_buf, x)
+        pre = pre_buf[x * C : (x + 1) * C, :]
+        back = summed(z_buf, x, ct_two, v_u)
         logistic = jax.nn.sigmoid(pre)
         keep = keep_buf[x * C : (x + 1) * C, :]
         value = (back * keep * logistic * (1.0 + pre * (1.0 - logistic))).astype(BF)
         v_i[(x + 1) * C : (x + 2) * C, 0:PLANE] = value
         for k in range(3):
             i_all[k * C : (k + 1) * C, (x + k) * PLANE : (x + k + 1) * PLANE] = value
-    pack_faces(v_i, 3)
-    sent.append(send_faces(3))
-
-    g_two = dot_nt(im_u[...], d_all[...])
-    g_full[0:288, 0:96] = g_two
-    g_full[0:288, 96:128] = jnp.zeros((288, 32), F32)
+
     g_one = dot_nt(i_all[...], im_f[...])
     g_full[288:384, :] = g_one[:, 0:128]
     g_full[384:480, :] = g_one[:, 128:256]
-    g_full[480:512, :] = jnp.concatenate(
-        [g_one[k * C : (k + 1) * C, 256:288] for k in range(3)] + [jnp.zeros((C, C), F32)], axis=1
-    )
-    g_send[...] = g_full[...].astype(BF)
-
-    def chunk(index):
-        return pl.ds(pl.multiple_of(index * 16, 16), 16)
-
-    def scatter_copy(o):
-        t = lax.rem(rank + o, group)
-        return pltpu.make_async_remote_copy(
-            src_ref=g_send.at[chunk(t), :],
-            dst_ref=g_slots.at[o],
-            send_sem=s1_send.at[o],
-            recv_sem=s1_recv.at[o],
-            device_id=at(ring * group + t),
-            device_id_type=MESH,
-        )
-
-    def ring_copy(o):
-        t = lax.rem(ring + o, rings)
-        return pltpu.make_async_remote_copy(
-            src_ref=z_slots.at[ring],
-            dst_ref=z_slots.at[ring],
-            send_sem=s2_send.at[o],
-            recv_sem=s2_recv.at[o],
-            device_id=at(t * group + rank),
-            device_id_type=MESH,
-        )
-
-    def gather_copy(o):
-        t = lax.rem(rank + o, group)
-        return pltpu.make_async_remote_copy(
-            src_ref=r_send,
-            dst_ref=fin.at[chunk(rank), :],
-            send_sem=s3_send.at[o],
-            recv_sem=s3_recv.at[o],
-            device_id=at(ring * group + t),
-            device_id_type=MESH,
-        )
-
-    def each(copy_of, upto, act):
-        def step(o, carry):
-            act(copy_of(o))
-            return carry
-
-        lax.fori_loop(1, upto, step, 0)
-
-    each(scatter_copy, group, lambda c: c.start())
+    centre = dot_nt(v_i[C : 2 * C, 0:PLANE], v_f[0 : 3 * C, 0:PLANE])
+    for x in range(1, EDGE):
+        centre = centre + dot_nt(
+            v_i[(x + 1) * C : (x + 2) * C, 0:PLANE], v_f[x * C : (x + 3) * C, 0:PLANE]
+        )
+    g_full[480:512, :] = jnp.concatenate([centre, jnp.zeros((C, C), F32)], axis=1)
+    g_send[288:512, :] = g_full[288:512, :].astype(BF)
+    for o in range(1, group):
+        scatter_copy(o).start()
+    pack_faces(v_i, 3)
+    sent.append(send_faces(3))
 
     shift_here(v_d, im_d)
-
-    each(scatter_copy, group, lambda c: c.wait_recv())
+    shift_here(v_i, im_i)
+
+    scattered.wait_recv()
     total = g_full[chunk(rank), :]
     for o in range(1, group):
         total = total + g_slots[o].astype(F32)
     z_slots[ring] = total
-    each(ring_copy, rings, lambda c: c.start())
-
-    shift_here(v_i, im_i)
+    for o in range(1, rings):
+        ring_copy(o).start()
 
     arrive(2)
     take_rims(v_d, im_d, 2)
     convolve(w_two, im_d, y_buf)
     for x in range(EDGE):
-        enc_ref[0, :, x * PLANE : (x + 1) * PLANE] = summed(y_buf, x).astype(BF)
-
-    each(ring_copy, rings, lambda c: c.wait_recv())
+        enc_ref[0, :, x * PLANE : (x + 1) * PLANE] = summed(y_buf, x, c_two, v_d).astype(BF)
+    out_enc = pltpu.make_async_copy(enc_ref, enc_hbm, out_sem.at[0])
+    out_enc.start()
+
+    ringed.wait_recv()
     total = z_slots[0]
     for o in range(1, rings):
         total = total + z_slots[o]
     r_send[...] = total.astype(BF)
     fin[chunk(rank), :] = total.astype(BF)
-    each(gather_copy, group, lambda c: c.start())
+    for o in range(1, group):
+        gather_copy(o).start()
 
     arrive(3)
     take_rims(v_i, im_i, 3)
     convolve(wt_one, im_i, z_buf)
     for x in range(EDGE):
-        gfeat_ref[0, :, x * PLANE : (x + 1) * PLANE] = summed(z_buf, x).astype(BF)
-
-    each(gather_copy, group, lambda c: c.wait_recv())
+        gfeat_ref[0, :, x * PLANE : (x + 1) * PLANE] = summed(z_buf, x, ct_one, v_i).astype(BF)
+    out_gfeat = pltpu.make_async_copy(gfeat_ref, gfeat_hbm, out_sem.at[1])
+    out_gfeat.start()
+
+    gathered.wait_recv()
+    out_fin = pltpu.make_async_copy(fin, fin_hbm, out_sem.at[2])
+    out_fin.start()
+
+    for pair in sent:
+        for copy in pair:
+            copy.wait_send()
+    scattered.wait_send()
+    ringed.wait_send()
+    gathered.wait_send()
+    for copy in (out_enc, out_gfeat, out_fin):
+        copy.wait()
+
+
+def write_out(
+    count,
+    enc_hbm,
+    gfeat_hbm,
+    fin_hbm,
+    enc_out,
+    gfeat_out,
+    one_out,
+    two_out,
+    enc_buf,
+    gfeat_buf,
+    fin,
+    one_buf,
+    two_buf,
+    sem,
+):
+    load_fin = pltpu.make_async_copy(fin_hbm, fin, sem.at[0])
+    load_enc = pltpu.make_async_copy(enc_hbm, enc_buf, sem.at[1])
+    load_gfeat = pltpu.make_async_copy(gfeat_hbm, gfeat_buf, sem.at[2])
+    for copy in (load_fin, load_enc, load_gfeat):
+        copy.start()
+    stores = [
+        pltpu.make_async_copy(one_buf, one_out, sem.at[3]),
+        pltpu.make_async_copy(two_buf, two_out, sem.at[4]),
+        pltpu.make_async_copy(enc_buf, enc_out, sem.at[5]),
+        pltpu.make_async_copy(gfeat_buf, gfeat_out, sem.at[6]),
+    ]
+    load_fin.wait()
     norm = F32(1.0 / math.sqrt(count * EDGE**3))
     for k in range(3):
         for s in range(9):
@@ -440,42 +546,48 @@
             else:
                 top, left = 480, k * C
             rows = fin[top : top + C, :].astype(F32)
-            gone_ref[k * 9 + s] = rows[:, left : left + C] * norm
+            one_buf[k * 9 + s] = rows[:, left : left + C] * norm
             rows = fin[q * C : (q + 1) * C, :].astype(F32)
-            gtwo_ref[k * 9 + s] = rows[:, (2 - k) * C : (3 - k) * C] * norm
-
-    for pair in sent:
-        for copy in pair:
-            copy.wait_send()
-    each(scatter_copy, group, lambda c: c.wait_send())
-    each(ring_copy, rings, lambda c: c.wait_send())
-    each(gather_copy, group, lambda c: c.wait_send())
+            two_buf[k * 9 + s] = rows[:, (2 - k) * C : (3 - k) * C] * norm
+    stores[0].start()
+    stores[1].start()
+    load_enc.wait()
+    stores[2].start()
+    load_gfeat.wait()
+    stores[3].start()
+    for copy in stores:
+        copy.wait()
 
 
 def local(count, *args):
     features, pool, skip, one, two, links, positions, seed = args
     shift = jnp.asarray(shift_matrices(), BF)
     face = jnp.asarray(face_matrix(), BF)
-    vmem = pl.BlockSpec(memory_space=pltpu.VMEM)
-    smem = pl.BlockSpec(memory_space=pltpu.SMEM)
     rows, lanes = SLABS * C, SLABS * PLANE
     dma = pltpu.SemaphoreType.DMA
     rings = count // 32
-    return pl.pallas_call(
+    hbm = pl.BlockSpec(memory_space=pltpu.HBM)
+    field = jax.ShapeDtypeStruct((1, C, EDGE**3), BF)
+    weight = jax.ShapeDtypeStruct((27, C, C), F32)
+    done = pl.pallas_call(
         functools.partial(kernel, count),
-        out_shape=(
-            jax.ShapeDtypeStruct((1, C, EDGE**3), BF),
-            jax.ShapeDtypeStruct((1, C, EDGE**3), BF),
-            jax.ShapeDtypeStruct((27, C, C), F32),
-            jax.ShapeDtypeStruct((27, C, C), F32),
-        ),
-        in_specs=[vmem] * 7 + [smem] * 3,
-        out_specs=(vmem,) * 4,
-        scratch_shapes=[pltpu.VMEM((rows, PLANE + 128), BF)] * 4
-        + [pltpu.VMEM((9 * C, lanes), BF)] * 4
-        + [pltpu.VMEM((96, 288), BF)] * 4
+        out_shape=(field, field, jax.ShapeDtypeStruct((512, 128), BF)),
+        in_specs=[hbm] * 10,
+        out_specs=(hbm,) * 3,
+        scratch_shapes=[pltpu.VMEM((1, C, EDGE**3), BF)] * 5
+        + [pltpu.VMEM((27, C, C), BF)] * 2
+        + [pltpu.VMEM((PLANE + 128, 8 * PLANE), BF), pltpu.VMEM((2 * PLANE, 128), BF)]
+        + [
+            pltpu.SMEM((1, 6), jnp.int32),
+            pltpu.SMEM((1, 3), jnp.int32),
+            pltpu.SMEM((1,), jnp.int32),
+        ]
+        + [pltpu.VMEM((rows, PLANE + 128), BF)] * 4
+        + [pltpu.VMEM((8 * C, lanes), BF)] * 4
+        + [pltpu.VMEM((96, 256), BF)] * 4
+        + [pltpu.VMEM((C, 96), BF)] * 4
         + [pltpu.VMEM((96, lanes), F32)] * 2
-        + [pltpu.VMEM((EDGE * C, PLANE), F32)]
+        + [pltpu.VMEM((EDGE * C, PLANE), F32)] * 2
         + [pltpu.VMEM((96, lanes), BF)] * 2
         + [pltpu.VMEM((4, 384, 128), BF)] * 3
         + [
@@ -485,22 +597,36 @@
             pltpu.VMEM((rings, 16, 128), F32),
             pltpu.VMEM((16, 128), BF),
             pltpu.VMEM((512, 128), BF),
+            dma((10,)),
+            dma((3,)),
             dma((8,)),
             dma((8,)),
-            dma((32,)),
-            dma((32,)),
-            dma((rings,)),
-            dma((rings,)),
-            dma((32,)),
-            dma((32,)),
+            dma((1,)),
+            dma((1,)),
+            dma((1,)),
+            dma((1,)),
+            dma((1,)),
+            dma((1,)),
         ],
         compiler_params=pltpu.CompilerParams(
-            collective_id=0, has_side_effects=True, vmem_limit_bytes=48 * 2**20
+            collective_id=0, has_side_effects=True, vmem_limit_bytes=64 * 2**20
         ),
         cost_estimate=pl.CostEstimate(
             flops=4_000_000_000, bytes_accessed=3_000_000, transcendentals=300_000
         ),
     )(features, pool, skip, one, two, shift, face, links, positions, seed)
+    return pl.pallas_call(
+        functools.partial(write_out, count),
+        out_shape=(field, field, weight, weight),
+        in_specs=[hbm] * 3,
+        out_specs=(hbm,) * 4,
+        scratch_shapes=[pltpu.VMEM((1, C, EDGE**3), BF)] * 2
+        + [pltpu.VMEM((512, 128), BF)]
+        + [pltpu.VMEM((27, C, C), F32)] * 2
+        + [dma((7,))],
+        compiler_params=pltpu.CompilerParams(vmem_limit_bytes=64 * 2**20),
+        cost_estimate=pl.CostEstimate(flops=0, bytes_accessed=2_000_000, transcendentals=0),
+    )(*done)
 
 
 def solution(mesh):

time: 53.7 us -> 42.5 us (0.79)
  local copies, waits for them, and re-layouts: 11.3 us -> 0 us
    unnamed x22 -> x0, local copies, waits for them, and re-layouts: 11.3 us -> none
    pallas_call x1 -> x2, Pallas kernels: 40.8 us -> 41.1 us  [the longest x1 38.8 us: local(): pl.pallas_call(functools.partial(kernel, count), out_shape=(field, field,...]
where the time goes in v2:
time: 42.5 us; the launch traced here: 42.4 us
  Pallas kernels  41.1 us (97%)
  between operations  1.29 us (3%)
    pallas_call x1, Pallas kernels, local(): pl.pallas_call(functools.partial(kernel, count), out_shape=(field, field,...  38.8 us
    pallas_call x1, Pallas kernels, local(): pl.pallas_call(functools.partial(write_out, count), out_shape=(field, fie...  2.27 us

profile of v2, /device:TPU:1, one launch (start us, length us, event | category | flops | bytes accessed | tf_op | source)
XLA Modules:
  0.0 42.4 jit_solution(6914676700701501564)
XLA Ops:
  1.3 38.8 %shard_map.129 = (bf16[1,32,4096]{2,1,0:T(8,128)(2,1)}, bf16[1,32,4096]{2,1,0:T(8,128)(2,1)}, bf16[512,128]{1,0:T(8,128)(2,1)}) custom-call(bf16[1,32,4096]{2,1,0:T(8,128)(2,1)} %feat_hbm.1, bf16[1,32,4096]{2,1,0:T(8,128)(2,1)} %pool_hbm.1, bf16[1,32,4096]{2,1,0:T(8,128)(2,1)} %skip_hbm.1, bf16[27,32,32]{2,1,0:T(8,128)(2,1)} %one_hbm.1, ...), custom_call_target="tpu_custom_call" | custom-call | flops 4000000000 | bytes 3000000 | tf_op jit(solution)/shard_map/pallas_call | solution.py:572
  40.1 2.3 %shard_map.130 = (bf16[1,32,4096]{2,1,0:T(8,128)(2,1)}, bf16[1,32,4096]{2,1,0:T(8,128)(2,1)}, f32[27,32,32]{2,1,0:T(8,128)}, f32[27,32,32]{2,1,0:T(8,128)}) custom-call(bf16[1,32,4096]{2,1,0:T(8,128)(2,1)} %get-tuple-element.7.enc_hbm, bf16[1,32,4096]{2,1,0:T(8,128)(2,1)} %get-tuple-element.8.gfeat_hbm, bf16[512,128]{1,0:T(8,128)(2,1)} %get-tuple-element.9.fin_hbm), custom_call_target="tpu_custom_call" | custom-call | bytes 2000000 | tf_op jit(solution)/shard_map/pallas_call | solution.py:618

commit v3 on v2

--- a/solution.py
+++ b/solution.py
@@ -54,6 +54,15 @@
             table[half * PLANE + i * EDGE + EDGE - 1, base + 2 * EDGE + i] = 1
             table[half * PLANE + i * EDGE, base + 3 * EDGE + i] = 1
     return table
+
+
+def far_first():
+    steps = [(x, c, y) for x in range(4) for c in range(2) for y in range(4)][1:]
+    return sorted(steps, key=lambda s: -(min(s[0], 4 - s[0]) + min(s[2], 4 - s[2]) + 0.1 * s[1]))
+
+
+STEPS = far_first()
+RING_STEPS = (4, 3, 5, 2, 6, 1, 7)
 
 
 def dot(a, b):
@@ -140,6 +149,14 @@
     rings = count // group
     ring, rank = me // group, lax.rem(me, group)
 
+    plane_x, core, plane_y = rank // 8, lax.rem(rank // 4, 2), lax.rem(rank, 4)
+
+    def member(o):
+        dx, dc, dy = STEPS[o - 1]
+        return (
+            lax.rem(plane_x + dx, 4) * 8 + lax.rem(core + dc, 2) * 4 + lax.rem(plane_y + dy, 4)
+        )
+
     def at(index):
         return (index // per, lax.rem(index, per))
 
@@ -169,9 +186,9 @@
         pl.semaphore_signal(barrier, inc=1, device_id=at(d), device_id_type=MESH)
 
     for o in range(1, group):
-        t = ring * group + lax.rem(rank + o, group)
+        t = ring * group + member(o)
         pl.semaphore_signal(barrier, inc=1, device_id=at(t), device_id_type=MESH)
-    for o in range(1, rings):
+    for o in RING_STEPS:
         t = lax.rem(ring + o, rings) * group + rank
         pl.semaphore_signal(barrier, inc=1, device_id=at(t), device_id_type=MESH)
 
@@ -179,13 +196,6 @@
     for x in range(EDGE):
         rows, lanes = pl.ds((x + 1) * C, C), pl.ds(x * PLANE, PLANE)
         v_f[rows, 0:PLANE] = feat_ref[0, :, lanes]
-    loads["pool"].wait()
-    loads["skip"].wait()
-    for x in range(EDGE):
-        rows, lanes = pl.ds((x + 1) * C, C), pl.ds(x * PLANE, PLANE)
-        v_u[rows, 0:PLANE] = (
-            pool_ref[0, :, lanes].astype(F32) + skip_ref[0, :, lanes].astype(F32)
-        ).astype(BF)
     zero = jnp.zeros((C, 128), BF)
     for v in (v_f, v_u, v_d, v_i):
         v[0:C, PLANE:] = zero
@@ -231,9 +241,18 @@
 
     loads["face"].wait()
     pack_faces(v_f, 0)
+    pl.semaphore_wait(barrier, 2 + (group - 1) + (rings - 1))
+    sent = [send_faces(0)]
+
+    loads["pool"].wait()
+    loads["skip"].wait()
+    for x in range(EDGE):
+        rows, lanes = pl.ds((x + 1) * C, C), pl.ds(x * PLANE, PLANE)
+        v_u[rows, 0:PLANE] = (
+            pool_ref[0, :, lanes].astype(F32) + skip_ref[0, :, lanes].astype(F32)
+        ).astype(BF)
     pack_faces(v_u, 1)
-    pl.semaphore_wait(barrier, 2 + (group - 1) + (rings - 1))
-    sent = [send_faces(0), send_faces(1)]
+    sent.append(send_faces(1))
 
     for name in ("one", "two", "links", "pos", "seed", "shift"):
         loads[name].wait()
@@ -298,6 +317,9 @@
 
     shift_here(v_f, im_f)
     shift_here(v_u, im_u)
+    for v, im in ((v_f, im_f), (v_u, im_u)):
+        for j in range(1, SLABS - 1):
+            im[8 * C :, j * PLANE : (j + 1) * PLANE] = v[j * C : (j + 1) * C, 0:PLANE]
 
     mlane = lax.broadcasted_iota(jnp.int32, (16, 128), 1)
     slot_of = lax.shift_right_logical(mlane, 4) & 3
@@ -330,6 +352,9 @@
         from_p, from_n = recvp[slot, 128:384, :], recvn[slot, 128:384, :]
         v[C : 9 * C, PLANE:] = from_p * p_low + from_n * n_low
         v[9 * C : 17 * C, PLANE:] = from_p * p_high + from_n * n_high
+        if im.shape[0] > 8 * C:
+            for j in (0, SLABS - 1):
+                im[8 * C :, j * PLANE : (j + 1) * PLANE] = v[j * C : (j + 1) * C, 0:PLANE]
         outer = jnp.concatenate([v[0:C, 0:PLANE], v[(SLABS - 1) * C :, 0:PLANE]], axis=0)
         for i in range(8):
             rim = dot(v[inner_rows, PLANE:], shift_ref[PLANE:, i * PLANE : (i + 1) * PLANE])
@@ -343,7 +368,7 @@
     def convolve(w, im, out):
         for j in range(0, SLABS, 2):
             lanes = pl.ds(j * PLANE, 2 * PLANE)
-            out[:, lanes] = dot(w[...], im[:, lanes])
+            out[:, lanes] = dot(w[...], im[0 : 8 * C, lanes])
 
     def summed(y, x, centre, v):
         return (
@@ -361,7 +386,7 @@
         return pl.ds(pl.multiple_of(index * 16, 16), 16)
 
     def scatter_copy(o):
-        t = lax.rem(rank + o, group)
+        t = member(o)
         return pltpu.make_async_remote_copy(
             src_ref=g_send.at[chunk(t), :],
             dst_ref=g_slots.at[o],
@@ -383,7 +408,7 @@
         )
 
     def gather_copy(o):
-        t = lax.rem(rank + o, group)
+        t = member(o)
         return pltpu.make_async_remote_copy(
             src_ref=r_send,
             dst_ref=fin.at[chunk(rank), :],
@@ -419,27 +444,23 @@
             d_all[k * C : (k + 1) * C, (x + k) * PLANE : (x + k + 1) * PLANE] = value
     pack_faces(v_d, 2)
     sent.append(send_faces(2))
+    for x in range(EDGE):
+        pre = pre_buf[x * C : (x + 1) * C, :]
+        logistic = jax.nn.sigmoid(pre)
+        keep = keep_buf[x * C : (x + 1) * C, :]
+        pre_buf[x * C : (x + 1) * C, :] = keep * logistic * (1.0 + pre * (1.0 - logistic))
 
     arrive(1)
     take_rims(v_u, im_u, 1)
 
-    g_two = dot_nt(d_all[...], im_u[...])
-    g_full[0:256, :] = jnp.transpose(jnp.concatenate([g_two, jnp.zeros((C, 256), F32)], axis=0))
-    centre = dot_nt(v_u[0:C, 0:PLANE], d_all[:, 0:PLANE])
-    for j in range(1, SLABS):
-        centre = centre + dot_nt(
-            v_u[j * C : (j + 1) * C, 0:PLANE], d_all[:, j * PLANE : (j + 1) * PLANE]
-        )
-    g_full[256:288, :] = jnp.concatenate([centre, jnp.zeros((C, C), F32)], axis=1)
+    g_two = dot_nt(im_u[...], d_all[...])
+    g_full[0:288, :] = jnp.concatenate([g_two, jnp.zeros((9 * C, C), F32)], axis=1)
     g_send[0:288, :] = g_full[0:288, :].astype(BF)
 
     convolve(wt_two, im_u, z_buf)
     for x in range(EDGE):
-        pre = pre_buf[x * C : (x + 1) * C, :]
         back = summed(z_buf, x, ct_two, v_u)
-        logistic = jax.nn.sigmoid(pre)
-        keep = keep_buf[x * C : (x + 1) * C, :]
-        value = (back * keep * logistic * (1.0 + pre * (1.0 - logistic))).astype(BF)
+        value = (back * pre_buf[x * C : (x + 1) * C, :]).astype(BF)
         v_i[(x + 1) * C : (x + 2) * C, 0:PLANE] = value
         for k in range(3):
             i_all[k * C : (k + 1) * C, (x + k) * PLANE : (x + k + 1) * PLANE] = value
@@ -447,12 +468,9 @@
     g_one = dot_nt(i_all[...], im_f[...])
     g_full[288:384, :] = g_one[:, 0:128]
     g_full[384:480, :] = g_one[:, 128:256]
-    centre = dot_nt(v_i[C : 2 * C, 0:PLANE], v_f[0 : 3 * C, 0:PLANE])
-    for x in range(1, EDGE):
-        centre = centre + dot_nt(
-            v_i[(x + 1) * C : (x + 2) * C, 0:PLANE], v_f[x * C : (x + 3) * C, 0:PLANE]
-        )
-    g_full[480:512, :] = jnp.concatenate([centre, jnp.zeros((C, C), F32)], axis=1)
+    g_full[480:512, :] = jnp.concatenate(
+        [g_one[k * C : (k + 1) * C, 256:288] for k in range(3)] + [jnp.zeros((C, C), F32)], axis=1
+    )
     g_send[288:512, :] = g_full[288:512, :].astype(BF)
     for o in range(1, group):
         scatter_copy(o).start()
@@ -467,7 +485,7 @@
     for o in range(1, group):
         total = total + g_slots[o].astype(F32)
     z_slots[ring] = total
-    for o in range(1, rings):
+    for o in RING_STEPS:
         ring_copy(o).start()
 
     arrive(2)
@@ -583,7 +601,8 @@
             pltpu.SMEM((1,), jnp.int32),
         ]
         + [pltpu.VMEM((rows, PLANE + 128), BF)] * 4
-        + [pltpu.VMEM((8 * C, lanes), BF)] * 4
+        + [pltpu.VMEM((9 * C, lanes), BF)] * 2
+        + [pltpu.VMEM((8 * C, lanes), BF)] * 2
         + [pltpu.VMEM((96, 256), BF)] * 4
         + [pltpu.VMEM((C, 96), BF)] * 4
         + [pltpu.VMEM((96, lanes), F32)] * 2

time: 42.5 us -> 40.9 us (0.962)
  Pallas kernels: 41.1 us -> 39.5 us
    pallas_call x1, Pallas kernels: 38.8 us -> 37.2 us  [local(): pl.pallas_call(functools.partial(kernel, count), out_shape=(field, field,...]
where the time goes in v3:
time: 40.9 us; the launch traced here: 40.8 us
  Pallas kernels  39.5 us (97%)
  between operations  1.29 us (3%)
    pallas_call x1, Pallas kernels, local(): pl.pallas_call(functools.partial(kernel, count), out_shape=(field, field,...  37.2 us
    pallas_call x1, Pallas kernels, local(): pl.pallas_call(functools.partial(write_out, count), out_shape=(field, fie...  2.27 us

profile of v3, /device:TPU:1, one launch (start us, length us, event | category | flops | bytes accessed | tf_op | source)
XLA Modules:
  0.0 40.8 jit_solution(10410923863298485371)
XLA Ops:
  1.3 37.2 %shard_map.129 = (bf16[1,32,4096]{2,1,0:T(8,128)(2,1)}, bf16[1,32,4096]{2,1,0:T(8,128)(2,1)}, bf16[512,128]{1,0:T(8,128)(2,1)}) custom-call(bf16[1,32,4096]{2,1,0:T(8,128)(2,1)} %feat_hbm.1, bf16[1,32,4096]{2,1,0:T(8,128)(2,1)} %pool_hbm.1, bf16[1,32,4096]{2,1,0:T(8,128)(2,1)} %skip_hbm.1, bf16[27,32,32]{2,1,0:T(8,128)(2,1)} %one_hbm.1, ...), custom_call_target="tpu_custom_call" | custom-call | flops 4000000000 | bytes 3000000 | tf_op jit(solution)/shard_map/pallas_call | solution.py:590
  38.5 2.3 %shard_map.130 = (bf16[1,32,4096]{2,1,0:T(8,128)(2,1)}, bf16[1,32,4096]{2,1,0:T(8,128)(2,1)}, f32[27,32,32]{2,1,0:T(8,128)}, f32[27,32,32]{2,1,0:T(8,128)}) custom-call(bf16[1,32,4096]{2,1,0:T(8,128)(2,1)} %get-tuple-element.7.enc_hbm, bf16[1,32,4096]{2,1,0:T(8,128)(2,1)} %get-tuple-element.8.gfeat_hbm, bf16[512,128]{1,0:T(8,128)(2,1)} %get-tuple-element.9.fin_hbm), custom_call_target="tpu_custom_call" | custom-call | bytes 2000000 | tf_op jit(solution)/shard_map/pallas_call | solution.py:637

commit v4 on v3

--- a/solution.py
+++ b/solution.py
@@ -131,6 +131,7 @@
     z_slots,
     r_send,
     fin,
+    know_sem,
     in_sem,
     out_sem,
     fsend_sem,
@@ -188,7 +189,7 @@
     for o in range(1, group):
         t = ring * group + member(o)
         pl.semaphore_signal(barrier, inc=1, device_id=at(t), device_id_type=MESH)
-    for o in RING_STEPS:
+    for o in (1, rings - 1):
         t = lax.rem(ring + o, rings) * group + rank
         pl.semaphore_signal(barrier, inc=1, device_id=at(t), device_id_type=MESH)
 
@@ -241,8 +242,15 @@
 
     loads["face"].wait()
     pack_faces(v_f, 0)
-    pl.semaphore_wait(barrier, 2 + (group - 1) + (rings - 1))
+    pl.semaphore_wait(barrier, 2 + (group - 1) + 2)
     sent = [send_faces(0)]
+
+    def tell(step, index):
+        for o in (step, rings - step):
+            t = lax.rem(ring + o, rings) * group + rank
+            pl.semaphore_signal(know_sem.at[index], inc=1, device_id=at(t), device_id_type=MESH)
+
+    tell(1, 0)
 
     loads["pool"].wait()
     loads["skip"].wait()
@@ -433,6 +441,8 @@
     gathered = all_of(g_slots.at[pl.ds(1, group - 1)], s3_send, s3_recv)
 
     arrive(0)
+    pl.semaphore_wait(know_sem.at[0], 2)
+    tell(2, 1)
     take_rims(v_f, im_f, 0)
     convolve(w_one, im_f, y_buf)
     for x in range(EDGE):
@@ -475,18 +485,19 @@
     for o in range(1, group):
         scatter_copy(o).start()
     pack_faces(v_i, 3)
-    sent.append(send_faces(3))
 
     shift_here(v_d, im_d)
     shift_here(v_i, im_i)
 
     scattered.wait_recv()
+    pl.semaphore_wait(know_sem.at[1], 2)
     total = g_full[chunk(rank), :]
     for o in range(1, group):
         total = total + g_slots[o].astype(F32)
     z_slots[ring] = total
     for o in RING_STEPS:
         ring_copy(o).start()
+    sent.append(send_faces(3))
 
     arrive(2)
     take_rims(v_d, im_d, 2)
@@ -616,6 +627,7 @@
             pltpu.VMEM((rings, 16, 128), F32),
             pltpu.VMEM((16, 128), BF),
             pltpu.VMEM((512, 128), BF),
+            pltpu.SemaphoreType.REGULAR((2,)),
             dma((10,)),
             dma((3,)),
             dma((8,)),

time: 40.9 us -> 40.3 us (0.985)
  Pallas kernels: 39.5 us -> 38.9 us
    pallas_call x1, Pallas kernels: 37.2 us -> 36.6 us  [local(): pl.pallas_call(functools.partial(kernel, count), out_shape=(field, field,...]
where the time goes in v4:
time: 40.3 us; the launch traced here: 40.2 us
  Pallas kernels  38.9 us (97%)
  between operations  1.29 us (3%)
    pallas_call x1, Pallas kernels, local(): pl.pallas_call(functools.partial(kernel, count), out_shape=(field, field,...  36.6 us
    pallas_call x1, Pallas kernels, local(): pl.pallas_call(functools.partial(write_out, count), out_shape=(field, fie...  2.27 us

profile of v4, /device:TPU:1, one launch (start us, length us, event | category | flops | bytes accessed | tf_op | source)
XLA Modules:
  0.0 40.2 jit_solution(6139645923585379483)
XLA Ops:
  1.3 36.6 %shard_map.129 = (bf16[1,32,4096]{2,1,0:T(8,128)(2,1)}, bf16[1,32,4096]{2,1,0:T(8,128)(2,1)}, bf16[512,128]{1,0:T(8,128)(2,1)}) custom-call(bf16[1,32,4096]{2,1,0:T(8,128)(2,1)} %feat_hbm.1, bf16[1,32,4096]{2,1,0:T(8,128)(2,1)} %pool_hbm.1, bf16[1,32,4096]{2,1,0:T(8,128)(2,1)} %skip_hbm.1, bf16[27,32,32]{2,1,0:T(8,128)(2,1)} %one_hbm.1, ...), custom_call_target="tpu_custom_call" | custom-call | flops 4000000000 | bytes 3000000 | tf_op jit(solution)/shard_map/pallas_call | solution.py:601
  37.9 2.3 %shard_map.130 = (bf16[1,32,4096]{2,1,0:T(8,128)(2,1)}, bf16[1,32,4096]{2,1,0:T(8,128)(2,1)}, f32[27,32,32]{2,1,0:T(8,128)}, f32[27,32,32]{2,1,0:T(8,128)}) custom-call(bf16[1,32,4096]{2,1,0:T(8,128)(2,1)} %get-tuple-element.7.enc_hbm, bf16[1,32,4096]{2,1,0:T(8,128)(2,1)} %get-tuple-element.8.gfeat_hbm, bf16[512,128]{1,0:T(8,128)(2,1)} %get-tuple-element.9.fin_hbm), custom_call_target="tpu_custom_call" | custom-call | bytes 2000000 | tf_op jit(solution)/shard_map/pallas_call | solution.py:649
